TPU v7x, 256 devices: a whole 4x4x8 slice. The times are simulated.
256 devices in a mesh: grp: 8 (over y, core), mem: 32 (over x, z).
Axes of the slice: x: 4, y: 4, z: 8, core: 2. Of those that a mesh axis runs over, the one named last changes fastest.
Arguments:
- old_rows: bfloat16 [65536, 1024], P(('grp', 'mem')), may hold values from -24 to 24
- new_rows: bfloat16 [65536, 1024], P(('grp', 'mem')), may hold values from -6 to 6
- list_ids: int32 [65536], P(('grp', 'mem')), may hold values from 0 to 65535, as said below
- owner_map: int32 [65536], replicated, may hold values from 0 to 31, as said below
Outputs:
- owner_rows: float32 [131072, 1024], P(('grp', 'mem'))
- rotation: bfloat16 [1024, 1024], P('mem')
Inputs may be any that keep to these rules, and one draw needn't show every extreme that they name: `list_ids`: in each device's block of 256 rows, at most 16 rows belong to lists of any one owner; in every group some owner receives exactly 16 rows from every device of the group. `owner_map`: every owner holds 65536 // 32 lists.
All inputs are finite; a program needn't handle non-finite values.
Results may differ from a plain program's by a relative error of at most 0.023.
Values may be sent and summed in bfloat16 or wider, within the bound.
No kernel may reach another device: no remote copies, remote signals or barrier semaphores. Data moves between devices by JAX's collectives and lax.ppermute only.
A program may use at most 64 MiB of HBM per device.

v0:
```python
import math
import jax
import jax.numpy as jnp
from jax import lax
from jax.sharding import PartitionSpec as P

ITERS = 2
EPSILON = 1e-06
COEFF_ONE = 3.4445
COEFF_THREE = -4.775
COEFF_FIVE = 2.0315


def combine_terms(iterate, first, second):
    return (
        COEFF_ONE * iterate.astype(jnp.float32)
        + COEFF_THREE * first.astype(jnp.float32)
        + COEFF_FIVE * second
    ).astype(jnp.bfloat16)


def local(old_rows, new_rows, list_ids, owner_map):
    features = old_rows.shape[1]
    row_total = old_rows.shape[0]
    members = lax.axis_size("mem")
    block_rows = features // members
    scaling = 0.25 * math.sqrt(features)
    partial_value = jnp.dot(old_rows.T, new_rows, preferred_element_type=jnp.float32)
    covariance = lax.psum(partial_value, ("grp", "mem"))
    squares = jnp.sum(covariance * covariance)
    iterate = (covariance * scaling / jnp.sqrt(squares + EPSILON)).astype(jnp.bfloat16)
    for sweep in range(ITERS):
        gram = jnp.dot(iterate, iterate.T, preferred_element_type=jnp.float32).astype(jnp.bfloat16)
        first = jnp.dot(gram, iterate, preferred_element_type=jnp.float32).astype(jnp.bfloat16)
        second = jnp.dot(gram, first, preferred_element_type=jnp.float32)
        iterate = combine_terms(iterate, first, second)
    own_rows = lax.dynamic_slice_in_dim(iterate, lax.axis_index("mem") * block_rows, block_rows, 0)
    capacity = 2 * row_total // members
    owner_of_row = owner_map[list_ids]
    onehot = (owner_of_row[:, None] == jnp.arange(members, dtype=jnp.int32)[None, :]).astype(
        jnp.int32
    )
    earlier = jnp.cumsum(onehot, axis=0) - onehot
    slot_index = owner_of_row * capacity + jnp.sum(earlier * onehot, axis=1)
    payload = jnp.dot(old_rows, iterate, preferred_element_type=jnp.float32)
    buffer = jnp.zeros((members * capacity, features), jnp.float32).at[slot_index].set(payload)
    buffer = buffer.reshape(members, capacity, features)
    arrived = lax.all_to_all(buffer, "mem", split_axis=0, concat_axis=0, tiled=True).reshape(
        members * capacity, features
    )
    return (arrived, own_rows)


def solution(mesh):
    in_specs = (P(("grp", "mem"), None), P(("grp", "mem"), None), P(("grp", "mem")), P())
    out_specs = (P(("grp", "mem"), None), P("mem", None))
    return jax.shard_map(local, mesh=mesh, in_specs=in_specs, out_specs=out_specs, check_vma=False)
```

profile of v0, /device:TPU:64, one launch (start us, length us, event | category | flops | bytes accessed | tf_op | source)
XLA Modules:
  0.0 378.5 jit_solution(7004765975214528384)
XLA Ops:
  7.2 0.0 copy-start
  7.2 0.0 all-reduce.2.cloned.1.call-start
  7.2 1.0 copy-done
  8.2 3.8 fusion.8
  12.0 0.0 copy-start.3
  12.0 0.0 copy-start.2
  12.0 0.0 all-reduce.2.cloned.1.call-update
  12.0 0.7 copy-done.3
  12.7 0.3 copy-done.2
  12.9 1.7 gather_fusion
  14.7 0.6 reduce-window.6
  15.3 0.2 slice_reduce_fusion
  15.5 0.1 fusion.6
  15.6 265.5 %all-reduce.2.cloned.1.call-done = f32[1024,1024]{1,0:T(8,128)} async-done(((f32[1024,1024]{1,0:T(8,128)}), f32[1024,1024]{1,0:T(8,128)}) %all-reduce.2.cloned.1.call-update) | async-done | bytes 4194320 | tf_op jit(solution)/shard_map/psum | solution.py:29
  281.1 3.9 %multiply_reduce_fusion = f32[]{:T(128)} fusion(f32[1024,1024]{1,0:T(8,128)} %all-reduce.2.cloned.1.call-done), kind=kLoop, calls=%fused_computation.5 | loop fusion | flops 2097151 | bytes 4194308 | tf_op jit(solution)/shard_map/reduce_sum | solution.py:30
  285.7 2.8 divide_convert_fusion
  288.5 2.4 convolution_convert_fusion.1
  290.9 2.3 fusion.9
  293.2 2.6 add_convert_fusion.1
  295.8 2.4 convolution_convert_fusion
  298.2 2.3 fusion.10
  300.5 2.8 add_convert_fusion
  303.3 0.0 copy-start.1
  303.3 1.3 copy-done.1
  304.7 0.8 convolution_bitcast_fusion
  305.5 0.3 copy.8
  305.8 2.8 scatter_custom_fusion
  308.6 11.8 %all-to-all-start = ((f32[32,16,1024]{2,1,0:T(8,128)}), f32[32,16,1024]{2,1,0:T(8,128)S(1)}, u32[]{:S(2)}, u32[]{:S(2)}) async-start(f32[32,16,1024]{2,1,0:T(8,128)} %bitcast.43), calls=%async_computation | async-start | bytes 4194304 | tf_op jit(solution)/shard_map/all_to_all | solution.py:48
  320.4 1.5 constant_dynamic-slice_fusion
  321.9 48.5 %all-to-all-done = f32[32,16,1024]{2,1,0:T(8,128)S(1)} async-done(((f32[32,16,1024]{2,1,0:T(8,128)}), f32[32,16,1024]{2,1,0:T(8,128)S(1)}, u32[]{:S(2)}, u32[]{:S(2)}) %all-to-all-start) | async-done | bytes 2097184 | tf_op jit(solution)/shard_map/all_to_all | solution.py:48
  370.4 1.3 copy.13
  (7 shorter events, 0.1 us)
Async XLA Ops:
  7.2 1.0 copy-start
  7.2 273.9 %all-reduce.2.cloned.1.call-start = ((), (), s32[]{:S(2)}) async-start(), calls=%async_computation.1 | async-start | bytes 8388608 | tf_op jit(solution)/shard_map/psum | solution.py:29
  12.0 0.7 copy-start.3
  12.0 1.0 copy-start.2
  303.3 1.4 copy-start.1
  308.6 61.7 %all-to-all-start = ((f32[32,16,1024]{2,1,0:T(8,128)}), f32[32,16,1024]{2,1,0:T(8,128)S(1)}, u32[]{:S(2)}, u32[]{:S(2)}) async-start(f32[32,16,1024]{2,1,0:T(8,128)} %bitcast.43), calls=%async_computation | async-start | bytes 4194304 | tf_op jit(solution)/shard_map/all_to_all | solution.py:48
Sparse Core Ops, SparseCore 0:
  13.5 267.5 all-reduce.1
where the time goes:
time: 379 us
  waiting for transfers between devices  314 us (83%)
  matrix products  19.3 us (5%)
  between operations  14.9 us (4%)
  starting transfers between devices  11.8 us (3%)
  local copies, waits for them, and re-layouts  11.1 us (3%)
  other arithmetic  7.41 us (2%)
    psum x1, waiting for transfers between devices, local(): covariance = lax.psum(partial_value, ('grp', 'mem'))  265 us
    all_to_all x1, waiting for transfers between devices, local(): lax.all_to_all(buffer, 'mem', split_axis=0, concat_axis=0, tiled=True)  48.5 us
    all_to_all x1, starting transfers between devices, local(): lax.all_to_all(buffer, 'mem', split_axis=0, concat_axis=0, tiled=True)  11.8 us
  transfers between devices with their start and end apart: 2, of which 2 were waited for; matrix products, arithmetic and copies ran while one was open for 1% of the time, Pallas kernels for 0%

commit v1 on v0

--- a/solution.py
+++ b/solution.py
@@ -26,7 +26,7 @@
     block_rows = features // members
     scaling = 0.25 * math.sqrt(features)
     partial_value = jnp.dot(old_rows.T, new_rows, preferred_element_type=jnp.float32)
-    covariance = lax.psum(partial_value, ("grp", "mem"))
+    covariance = lax.psum(lax.psum(partial_value, "grp"), "mem")
     squares = jnp.sum(covariance * covariance)
     iterate = (covariance * scaling / jnp.sqrt(squares + EPSILON)).astype(jnp.bfloat16)
     for sweep in range(ITERS):

time: 379 us -> 351 us (0.926)
  waiting for transfers between devices: 314 us -> 289 us
  starting transfers between devices: 11.8 us -> 6.48 us
    psum x1 -> x2, waiting for transfers between devices: 265 us -> 244 us  [local(): covariance = lax.psum(lax.psum(partial_value, 'grp'), 'mem')]
    all_to_all x1, starting transfers between devices: 11.8 us -> 6.4 us  [local(): lax.all_to_all(buffer, 'mem', split_axis=0, concat_axis=0, tiled=True)]
  transfers between devices with their start and end apart: 2 -> 3, of which waited for: 2 -> 3; matrix products, arithmetic and copies ran while one was open for 1% -> 1% of each run, Pallas kernels for 0% -> 0%
where the time goes in v1:
time: 351 us; the launch traced here: 348 us
  waiting for transfers between devices  289 us (82%)
  matrix products  19.3 us (5%)
  between operations  14.9 us (4%)
  local copies, waits for them, and re-layouts  11.1 us (3%)
  other arithmetic  7.41 us (2%)
  starting transfers between devices  6.48 us (2%)
    psum x2, waiting for transfers between devices, local(): covariance = lax.psum(lax.psum(partial_value, 'grp'), 'mem')  244 us
    all_to_all x1, waiting for transfers between devices, local(): lax.all_to_all(buffer, 'mem', split_axis=0, concat_axis=0, tiled=True)  45 us
  transfers between devices with their start and end apart: 3, of which 3 were waited for; matrix products, arithmetic and copies ran while one was open for 1% of the time, Pallas kernels for 0%

profile of v1, /device:TPU:64, one launch (start us, length us, event | category | flops | bytes accessed | tf_op | source)
XLA Modules:
  0.0 347.9 jit_solution(5141302006036730443)
XLA Ops:
  7.2 0.0 copy-start
  7.2 0.0 all-reduce.3.cloned.1.call-start
  7.2 1.0 copy-done
  8.2 3.8 %fusion.8 = f32[1024,1024]{1,0:T(8,128)} fusion(bf16[256,1024]{1,0:T(8,128)(2,1)S(1)} %copy-done, bf16[256,1024]{1,0:T(8,128)(2,1)} %param.5), kind=kOutput, calls=%fused_computation.27 | convolution fusion | flops 536870912 | bytes 5242880 | tf_op jit(solution)/shard_map/dot_general | solution.py:28
  12.0 0.0 all-reduce.3.cloned.1.call-update
  12.0 0.0 all-reduce.5.cloned.1.call-start
  12.0 80.0 %all-reduce.3.cloned.1.call-done = f32[1024,1024]{1,0:T(8,128)} async-done(((f32[1024,1024]{1,0:T(8,128)}), f32[1024,1024]{1,0:T(8,128)}) %all-reduce.3.cloned.1.call-update) | async-done | bytes 4194320 | tf_op jit(solution)/shard_map/psum | solution.py:29
  92.0 0.0 copy-start.3
  92.0 0.0 copy-start.2
  92.0 0.0 all-reduce.5.cloned.1.call-update
  92.0 0.7 copy-done.3
  92.7 0.3 copy-done.2
  93.0 1.7 gather_fusion
  94.7 0.6 reduce-window.6
  95.3 0.2 slice_reduce_fusion
  95.6 0.1 fusion.6
  95.7 163.6 %all-reduce.5.cloned.1.call-done = f32[1024,1024]{1,0:T(8,128)} async-done(((f32[1024,1024]{1,0:T(8,128)}), f32[1024,1024]{1,0:T(8,128)}) %all-reduce.5.cloned.1.call-update) | async-done | bytes 4194320 | tf_op jit(solution)/shard_map/psum | solution.py:29
  259.3 3.9 %multiply_reduce_fusion = f32[]{:T(128)} fusion(f32[1024,1024]{1,0:T(8,128)} %all-reduce.5.cloned.1.call-done), kind=kLoop, calls=%fused_computation.5 | loop fusion | flops 2097151 | bytes 4194308 | tf_op jit(solution)/shard_map/reduce_sum | solution.py:30
  263.9 2.8 divide_convert_fusion
  266.7 2.4 convolution_convert_fusion.1
  269.0 2.3 fusion.9
  271.4 2.6 add_convert_fusion.1
  274.0 2.4 convolution_convert_fusion
  276.4 2.3 fusion.10
  278.7 2.8 add_convert_fusion
  281.5 0.0 copy-start.1
  281.5 1.3 copy-done.1
  282.9 0.8 convolution_bitcast_fusion
  283.6 0.3 copy.8
  284.0 2.8 scatter_custom_fusion
  286.8 6.4 %all-to-all-start = ((f32[32,16,1024]{2,1,0:T(8,128)}), f32[32,16,1024]{2,1,0:T(8,128)S(1)}, u32[]{:S(2)}, u32[]{:S(2)}) async-start(f32[32,16,1024]{2,1,0:T(8,128)} %bitcast.43), calls=%async_computation | async-start | bytes 4194304 | tf_op jit(solution)/shard_map/all_to_all | solution.py:48
  293.2 1.5 constant_dynamic-slice_fusion
  294.7 45.0 %all-to-all-done = f32[32,16,1024]{2,1,0:T(8,128)S(1)} async-done(((f32[32,16,1024]{2,1,0:T(8,128)}), f32[32,16,1024]{2,1,0:T(8,128)S(1)}, u32[]{:S(2)}, u32[]{:S(2)}) %all-to-all-start) | async-done | bytes 2097184 | tf_op jit(solution)/shard_map/all_to_all | solution.py:48
  339.7 1.3 copy.14
  (7 shorter events, 0.1 us)
Async XLA Ops:
  7.2 1.0 copy-start
  7.2 84.8 %all-reduce.3.cloned.1.call-start = ((), (), s32[]{:S(2)}) async-start(), calls=%async_computation.1 | async-start | bytes 8388608 | tf_op jit(solution)/shard_map/psum | solution.py:29
  12.0 247.3 %all-reduce.5.cloned.1.call-start = ((), (), s32[]{:S(2)}) async-start(), calls=%async_computation.2 | async-start | bytes 8388608 | tf_op jit(solution)/shard_map/psum | solution.py:29
  92.0 0.7 copy-start.3
  92.0 1.0 copy-start.2
  281.5 1.4 copy-start.1
  286.8 52.9 %all-to-all-start = ((f32[32,16,1024]{2,1,0:T(8,128)}), f32[32,16,1024]{2,1,0:T(8,128)S(1)}, u32[]{:S(2)}, u32[]{:S(2)}) async-start(f32[32,16,1024]{2,1,0:T(8,128)} %bitcast.43), calls=%async_computation | async-start | bytes 4194304 | tf_op jit(solution)/shard_map/all_to_all | solution.py:48
Sparse Core Ops, SparseCore 0:
  12.1 79.8 all-reduce.2
  95.6 163.6 all-reduce.4
